TPU v7x, 32 devices: a whole 2x2x4 slice. The times are simulated.
32 devices in a mesh: mem: 8 (over z, x), pb: 4 (over y, core).
Axes of the slice: x: 2, y: 2, z: 4, core: 2. Of those that a mesh axis runs over, the one named last changes fastest.
Arguments:
- query_raw: bfloat16 [1024, 5120], P('mem', 'pb'), may hold values from -420 to 420
- query_tangent: bfloat16 [1024, 5120], P('mem', 'pb'), may hold values from -6 to 6
- norm_gain: float32 [5120], P('pb'), may hold values from 0.1 to 1.9
- mem_keys: bfloat16 [4096, 5120], P('mem', 'pb'), may hold values from -110 to 110
- mem_values: bfloat16 [4096, 5120], P('mem', 'pb'), may hold values from -6 to 6
- retrieved: int32 [256, 4], P('mem'), may hold values from 0 to 7, all different within a row; in each aligned block of 32 rows (0 to 31, 32 to 63, ...) at most 32 rows name the same one
Outputs:
- attended: bfloat16 [1024, 5120], P('mem', 'pb')
- attended_tangent: bfloat16 [1024, 5120], P('mem', 'pb')
Inputs may be any that keep to these rules, and one draw needn't show every extreme that they name: `retrieved`: each row names 4 different frames; among the 32 rows of one index of mem no frame is named by more than 32 rows, a bound that some block reaches of them.
All inputs are finite; a program needn't handle non-finite values.
Results may differ from a plain program's by a relative error of at most 0.0055.
The roundings to bfloat16 on the way count: a program that leaves them out, or rounds other values in their place, can miss the bound.
Values may be sent and summed in bfloat16 or wider, within the bound.
A program may use at most 64 MiB of HBM per device.

v0:
```python
import math

import jax
import jax.numpy as jnp
from jax import lax
from jax.sharding import PartitionSpec as P

HEADS = 40
HDIM = 128
QBLK = 4


EPSILON = 1e-06


def head_partials(query_rows, tangent_rows, mem_keys, mem_values, head_count):
    row_count = query_rows.shape[0]
    score_scale = 1.0 / math.sqrt(HDIM)
    feature_width = head_count * HDIM
    dims_spec = (((1,), (1,)), ((), ()))

    def head_step(head_index, carry):
        start = head_index * HDIM
        query_head = lax.dynamic_slice_in_dim(query_rows, start, HDIM, 1)
        key_head = lax.dynamic_slice_in_dim(mem_keys, start, HDIM, 1)
        value_head = lax.dynamic_slice_in_dim(mem_values, start, HDIM, 1)
        scores = (
            lax.dot_general(query_head, key_head, dims_spec, preferred_element_type=jnp.float32)
            * score_scale
        )
        peak = jnp.max(scores, axis=1)
        weights = jnp.exp(scores - peak[:, None])
        updated = list(carry)
        total = jnp.sum(weights, axis=1)
        out_head = jnp.dot(
            weights.astype(jnp.bfloat16), value_head, preferred_element_type=jnp.float32
        ).astype(jnp.bfloat16)
        updated[0] = lax.dynamic_update_slice_in_dim(carry[0], out_head, start, 1)
        updated[1] = lax.dynamic_update_slice_in_dim(carry[1], peak[:, None], head_index, 1)
        updated[2] = lax.dynamic_update_slice_in_dim(carry[2], total[:, None], head_index, 1)
        tangent_head = lax.dynamic_slice_in_dim(tangent_rows, start, HDIM, 1)
        dscores = (
            lax.dot_general(tangent_head, key_head, dims_spec, preferred_element_type=jnp.float32)
            * score_scale
        )
        drift = weights * dscores
        drift_total = jnp.sum(drift, axis=1)
        tangent_out = jnp.dot(
            drift.astype(jnp.bfloat16), value_head, preferred_element_type=jnp.float32
        ).astype(jnp.bfloat16)
        updated[3] = lax.dynamic_update_slice_in_dim(carry[3], tangent_out, start, 1)
        updated[4] = lax.dynamic_update_slice_in_dim(carry[4], drift_total[:, None], head_index, 1)
        return tuple(updated)

    stat_zeros = jnp.zeros((row_count, head_count), jnp.float32)
    wide_zeros = jnp.zeros((row_count, feature_width), jnp.bfloat16)
    initial = (wide_zeros, stat_zeros, stat_zeros, wide_zeros, stat_zeros)
    return lax.fori_loop(0, head_count, head_step, initial)


def local(query_raw, query_tangent, norm_gain, mem_keys, mem_values, retrieved):
    owners = lax.axis_size("mem")
    block_count, pick_count = retrieved.shape
    token_count, feature_width = query_raw.shape
    head_count = feature_width // HDIM
    capacity = max(2, 2 * block_count * pick_count // owners)
    values_f = query_raw.astype(jnp.float32)
    tangent_f = query_tangent.astype(jnp.float32)
    square_sum, cross_sum = lax.psum(
        (jnp.sum(values_f * values_f, axis=1), jnp.sum(values_f * tangent_f, axis=1)), "pb"
    )
    full_width = HEADS * HDIM
    inverse = lax.rsqrt(square_sum / full_width + EPSILON)[:, None]
    cross_mean = (cross_sum / full_width)[:, None]
    normed = (values_f * inverse * norm_gain).astype(jnp.bfloat16)
    normed_tangent = (
        norm_gain * (tangent_f * inverse - values_f * (inverse**3 * cross_mean))
    ).astype(jnp.bfloat16)
    flat_ids = retrieved.reshape(-1)
    one_hot = (flat_ids[:, None] == jnp.arange(owners, dtype=jnp.int32)[None, :]).astype(jnp.int32)
    earlier = jnp.cumsum(one_hot, axis=0) - one_hot
    position = jnp.sum(earlier * one_hot, axis=1)
    target = flat_ids * capacity + position

    def pack(rows_in):
        copies = jnp.repeat(rows_in.reshape(block_count, QBLK, feature_width), pick_count, axis=0)
        buffer_rows = (
            jnp.zeros((owners * capacity, QBLK, feature_width), jnp.bfloat16).at[target].set(copies)
        )
        return buffer_rows.reshape(owners, capacity * QBLK, feature_width)

    send_query = pack(normed)
    send_tangent = pack(normed_tangent)

    def flatten(piece):
        return piece.reshape(-1, piece.shape[-1])

    def unflatten(array, sources, slot_rows):
        return array.reshape(sources, slot_rows, array.shape[-1])

    pieces = (
        lax.all_to_all(send_query, "mem", split_axis=0, concat_axis=0, tiled=True),
        lax.all_to_all(send_tangent, "mem", split_axis=0, concat_axis=0, tiled=True),
    )
    sources, slot_rows, _unused = pieces[0].shape
    out_part, peak_part, total_part, tangent_part, drift_part = head_partials(
        flatten(pieces[0]), flatten(pieces[1]), mem_keys, mem_values, head_count
    )
    partial_out = lax.all_to_all(
        unflatten(out_part, sources, slot_rows).astype(jnp.float32),
        "mem",
        split_axis=0,
        concat_axis=0,
        tiled=True,
    ).astype(jnp.bfloat16)
    peaks = lax.all_to_all(
        unflatten(peak_part, sources, slot_rows), "mem", split_axis=0, concat_axis=0, tiled=True
    )
    totals = lax.all_to_all(
        unflatten(total_part, sources, slot_rows), "mem", split_axis=0, concat_axis=0, tiled=True
    )
    partial_tangent = lax.all_to_all(
        unflatten(tangent_part, sources, slot_rows).astype(jnp.float32),
        "mem",
        split_axis=0,
        concat_axis=0,
        tiled=True,
    ).astype(jnp.bfloat16)
    drifts = lax.all_to_all(
        unflatten(drift_part, sources, slot_rows), "mem", split_axis=0, concat_axis=0, tiled=True
    )

    def pick_rows(array, trailing):
        slots = array.reshape((owners * capacity, QBLK) + trailing)
        return slots[target].reshape((block_count, pick_count, QBLK) + trailing)

    out_picked = pick_rows(partial_out, (head_count, HDIM))
    tangent_picked = pick_rows(partial_tangent, (head_count, HDIM))
    peak_picked = pick_rows(peaks, (head_count,))
    total_picked = pick_rows(totals, (head_count,))
    drift_picked = pick_rows(drifts, (head_count,))
    top = jnp.max(peak_picked, axis=1)
    factor = jnp.exp(peak_picked - top[:, None])
    merged_total = jnp.sum(factor * total_picked, axis=1)[..., None]
    merged_drift = jnp.sum(factor * drift_picked, axis=1)[..., None]
    merged = jnp.sum(factor[..., None] * out_picked.astype(jnp.float32), axis=1)
    merged_tangent = jnp.sum(factor[..., None] * tangent_picked.astype(jnp.float32), axis=1)
    attended = merged / merged_total
    attended_tangent = merged_tangent / merged_total - merged_drift / merged_total * attended
    return (
        attended.astype(jnp.bfloat16).reshape(token_count, feature_width),
        attended_tangent.astype(jnp.bfloat16).reshape(token_count, feature_width),
    )


def solution(mesh):
    placed = (
        P("mem", "pb"),
        P("mem", "pb"),
        P("pb"),
        P("mem", "pb"),
        P("mem", "pb"),
        P("mem", None),
    )
    return jax.shard_map(
        local,
        mesh=mesh,
        in_specs=placed,
        out_specs=(P("mem", "pb"), P("mem", "pb")),
        check_vma=False,
    )
```

profile of v0, /device:TPU:0, one launch (start us, length us, event | category | flops | bytes accessed | tf_op | source)
XLA Modules:
  0.0 408.4 jit_solution(16958528169024114098)
XLA Ops:
  4.1 8.4 %all-reduce = (f32[128]{0:T(128)S(1)}, f32[128]{0:T(128)S(1)}) all-reduce(f32[128]{0:T(128)S(1)} %get-tuple-element.181, f32[128]{0:T(128)S(1)} %get-tuple-element.180), channel_id=1, replica_groups=mesh['mem'=8,'pb'=4] {'pb'}, use_global_device_ids=true, to_apply=%region_3.0 | all-reduce | flops 256 | bytes 2048 | tf_op jit(solution)/shard_map/psum | solution.py:69
  16.1 11.6 %scatter_fusion = bf16[256,4,1280]{2,1,0:T(4,128)(2,1)S(1)} fusion(bf16[256,4,1280]{2,1,0:T(4,128)(2,1)S(1)} %broadcast.61.clone, s32[128]{0:T(128)S(1)} %fusion.33, bf16[128,4,1280]{2,1,0:T(4,128)(2,1)} %bitcast.73), kind=kCustom, calls=%fused_computation.5 | custom fusion | bytes 3932672 | tf_op jit(solution)/shard_map/scatter | solution.py:88
  29.9 5.8 %all-to-all-start = ((bf16[8,128,1280]{2,1,0:T(8,128)(2,1)}), bf16[8,128,1280]{2,1,0:T(8,128)(2,1)}, u32[]{:S(2)}, u32[]{:S(2)}) async-start(bf16[8,128,1280]{2,1,0:T(8,128)(2,1)} %reshape.141), calls=%async_computation | async-start | bytes 5242880 | tf_op jit(solution)/shard_map/all_to_all | solution.py:102
  37.9 11.6 %scatter_fusion.1 = bf16[256,4,1280]{2,1,0:T(4,128)(2,1)S(1)} fusion(bf16[256,4,1280]{2,1,0:T(4,128)(2,1)S(1)} %broadcast.61.clone.1, s32[128]{0:T(128)S(1)} %fusion.33, bf16[128,4,1280]{2,1,0:T(4,128)(2,1)} %bitcast.74), kind=kCustom, calls=%fused_computation.6 | custom fusion | bytes 3932672 | tf_op jit(solution)/shard_map/scatter | solution.py:88
  49.5 2.3 reshape.145
  51.8 42.3 %all-to-all-done = bf16[8,128,1280]{2,1,0:T(8,128)(2,1)} async-done(((bf16[8,128,1280]{2,1,0:T(8,128)(2,1)}), bf16[8,128,1280]{2,1,0:T(8,128)(2,1)}, u32[]{:S(2)}, u32[]{:S(2)}) %all-to-all-start) | async-done | bytes 2621472 | tf_op jit(solution)/shard_map/all_to_all | solution.py:102
  94.1 4.4 %all-to-all-start.1 = ((bf16[8,128,1280]{2,1,0:T(8,128)(2,1)}), bf16[8,128,1280]{2,1,0:T(8,128)(2,1)}, u32[]{:S(2)}, u32[]{:S(2)}) async-start(bf16[8,128,1280]{2,1,0:T(8,128)(2,1)} %reshape.145), calls=%async_computation.1 | async-start | bytes 5242880 | tf_op jit(solution)/shard_map/all_to_all | solution.py:103
  98.5 59.0 %all-to-all-done.1 = bf16[8,128,1280]{2,1,0:T(8,128)(2,1)} async-done(((bf16[8,128,1280]{2,1,0:T(8,128)(2,1)}), bf16[8,128,1280]{2,1,0:T(8,128)(2,1)}, u32[]{:S(2)}, u32[]{:S(2)}) %all-to-all-start.1) | async-done | bytes 2621472 | tf_op jit(solution)/shard_map/all_to_all | solution.py:103
  160.8 81.3 %while.21 = (s32[]{:T(128)}, bf16[1024,1280]{1,0:T(8,128)(2,1)}, f32[1024,10]{0,1:T(8,128)S(1)}, f32[1024,10]{0,1:T(8,128)S(1)}, bf16[1024,1280]{1,0:T(8,128)(2,...) while((s32[]{:T(128)}, bf16[1024,1280]{1,0:T(8,128)(2,1)}, ...), condition=%wide.region_12.13_spmd, body=%wide.region_8.12_spmd.sunk | while | flops 544470016 | bytes 12112071 | solution.py:58
  162.3 2.2 fusion.49
  178.6 2.2 fusion.49
  242.8 3.6 all-to-all-start.6
  247.1 6.2 %all-to-all-done.6 = f32[8,128,10]{1,2,0:T(8,128)S(1)} async-done(((f32[8,128,10]{1,2,0:T(8,128)}), f32[8,128,10]{1,2,0:T(8,128)S(1)}, u32[]{:S(2)}, u32[]{:S(2)}) %all-to-all-start.6) | async-done | bytes 40992 | tf_op jit(solution)/shard_map/all_to_all | solution.py:129
  253.3 3.4 all-to-all-start.4
  256.7 6.8 %all-to-all-done.4 = f32[8,128,10]{1,2,0:T(8,128)S(1)} async-done(((f32[8,128,10]{1,2,0:T(8,128)}), f32[8,128,10]{1,2,0:T(8,128)S(1)}, u32[]{:S(2)}, u32[]{:S(2)}) %all-to-all-start.4) | async-done | bytes 40992 | tf_op jit(solution)/shard_map/all_to_all | solution.py:119
  263.5 9.3 %all_to_all.35 = f32[8,128,10]{1,2,0:T(8,128)S(1)} all-to-all(f32[8,128,10]{1,2,0:T(8,128)S(1)} %copy.23), channel_id=1, replica_groups=mesh['mem'=8,'pb'=4] {'mem'}, dimensions={0} | all-to-all | bytes 81920 | tf_op jit(solution)/shard_map/all_to_all | solution.py:116
  272.8 60.7 %all_to_all.36 = bf16[8,128,1280]{2,1,0:T(8,128)(2,1)} all-to-all(bf16[8,128,1280]{2,1,0:T(8,128)(2,1)} %bitcast.72), channel_id=1, replica_groups=mesh['mem'=8,'pb'=4] {'mem'}, dimensions={0} | all-to-all | bytes 5242880 | tf_op jit(solution)/shard_map/all_to_all | solution.py:122
  333.6 3.8 all-to-all-start.3
  343.1 6.3 %reshape.154 = bf16[256,4,10,128]{3,2,1,0:T(8,128)(2,1)} reshape(bf16[8,128,1280]{2,1,0:T(8,128)(2,1)} %all_to_all.36) | data formatting | bytes 5242880 | tf_op jit(solution)/shard_map/reshape | solution.py:134
  349.4 4.3 %gather_fusion.3 = bf16[128,4,10,128]{3,2,1,0:T(8,128)(2,1)} fusion(bf16[256,4,10,128]{3,2,1,0:T(8,128)(2,1)} %reshape.154, s32[1024]{0:T(1024)S(1)} %pad_clamp_fusion), kind=kCustom, calls=%fused_computation.3 | custom fusion | bytes 2621952 | tf_op jit(solution)/shard_map/gather | solution.py:135
  353.8 41.8 %all-to-all-done.3 = bf16[8,128,1280]{2,1,0:T(8,128)(2,1)S(1)} async-done(((bf16[8,128,1280]{2,1,0:T(8,128)(2,1)}), bf16[8,128,1280]{2,1,0:T(8,128)(2,1)S(1)}, u32[]{:S(2)}, u32[]{:S(2)}) %all-to-all-start.3) | async-done | bytes 2621472 | tf_op jit(solution)/shard_map/all_to_all | solution.py:109
  395.5 3.3 reshape.150
  398.8 4.5 %gather_fusion.1 = bf16[128,4,10,128]{3,2,1,0:T(8,128)(2,1)} fusion(bf16[256,4,10,128]{3,2,1,0:T(8,128)(2,1)} %reshape.150, s32[1024]{0:T(1024)S(1)} %pad_clamp_fusion), kind=kCustom, calls=%fused_computation.1 | custom fusion | bytes 2621952 | tf_op jit(solution)/shard_map/gather | solution.py:135
  403.3 3.4 fusion.20
  (125 shorter events, 99.8 us)
Async XLA Ops:
  29.9 64.2 %all-to-all-start = ((bf16[8,128,1280]{2,1,0:T(8,128)(2,1)}), bf16[8,128,1280]{2,1,0:T(8,128)(2,1)}, u32[]{:S(2)}, u32[]{:S(2)}) async-start(bf16[8,128,1280]{2,1,0:T(8,128)(2,1)} %reshape.141), calls=%async_computation | async-start | bytes 5242880 | tf_op jit(solution)/shard_map/all_to_all | solution.py:102
  94.1 63.4 %all-to-all-start.1 = ((bf16[8,128,1280]{2,1,0:T(8,128)(2,1)}), bf16[8,128,1280]{2,1,0:T(8,128)(2,1)}, u32[]{:S(2)}, u32[]{:S(2)}) async-start(bf16[8,128,1280]{2,1,0:T(8,128)(2,1)} %reshape.145), calls=%async_computation.1 | async-start | bytes 5242880 | tf_op jit(solution)/shard_map/all_to_all | solution.py:103
  242.8 10.5 %all-to-all-start.6 = ((f32[8,128,10]{1,2,0:T(8,128)}), f32[8,128,10]{1,2,0:T(8,128)S(1)}, u32[]{:S(2)}, u32[]{:S(2)}) async-start(f32[8,128,10]{1,2,0:T(8,128)} %copy.27), calls=%async_computation.6 | async-start | bytes 131072 | tf_op jit(solution)/shard_map/all_to_all | solution.py:129
  253.3 10.2 %all-to-all-start.4 = ((f32[8,128,10]{1,2,0:T(8,128)}), f32[8,128,10]{1,2,0:T(8,128)S(1)}, u32[]{:S(2)}, u32[]{:S(2)}) async-start(f32[8,128,10]{1,2,0:T(8,128)} %copy.25), calls=%async_computation.4 | async-start | bytes 131072 | tf_op jit(solution)/shard_map/all_to_all | solution.py:119
  333.6 62.0 %all-to-all-start.3 = ((bf16[8,128,1280]{2,1,0:T(8,128)(2,1)}), bf16[8,128,1280]{2,1,0:T(8,128)(2,1)S(1)}, u32[]{:S(2)}, u32[]{:S(2)}) async-start(bf16[8,128,1280]{2,1,0:T(8,128)(2,1)} %bitcast.71), calls=%async_computation.3 | async-start | bytes 5242880 | tf_op jit(solution)/shard_map/all_to_all | solution.py:109
  398.8 4.5 %copy-start = (bf16[128,4,10,128]{3,2,1,0:T(8,128)(2,1)S(1)}, bf16[128,4,10,128]{3,2,1,0:T(8,128)(2,1)}, u32[]{:S(2)}) copy-start(bf16[128,4,10,128]{3,2,1,0:T(8,128)(2,1)} %gather_fusion.3) | copy-start | bytes 3932164
where the time goes:
time: 411 us; the launch traced here: 408 us
  waiting for transfers between devices  156 us (38%)
  blocking collectives  78.4 us (19%)
  matrix products  74.6 us (18%)
  local copies, waits for them, and re-layouts  64 us (16%)
  starting transfers between devices  21 us (5%)
  other arithmetic  13 us (3%)
    all_to_all x1, blocking collectives, local(): lax.all_to_all(unflatten(tangent_part, sources, slot_rows).astype(jnp.flo...  60.7 us
    all_to_all x1, waiting for transfers between devices, local(): lax.all_to_all(send_tangent, 'mem', split_axis=0, concat_axis=0, tiled=True)  59 us
    all_to_all x1, waiting for transfers between devices, local(): lax.all_to_all(send_query, 'mem', split_axis=0, concat_axis=0, tiled=True)  42.3 us
    all_to_all x1, waiting for transfers between devices, local(): lax.all_to_all(unflatten(out_part, sources, slot_rows).astype(jnp.float32...  41.8 us
    scatter x2, local copies, waits for them, and re-layouts, pack(): jnp.zeros((owners * capacity, QBLK, feature_width), jnp.bfloat16).at[target]  23.2 us
    dot_general x10, matrix products, head_step(): jnp.dot(weights.astype(jnp.bfloat16), value_head, preferred_element_type=...  22.3 us
    dot_general x10, matrix products, head_step(): jnp.dot(drift.astype(jnp.bfloat16), value_head, preferred_element_type=jn...  21.6 us
    dot_general x10, matrix products, head_step(): lax.dot_general(tangent_head, key_head, dims_spec, preferred_element_type...  16.4 us
  transfers between devices with their start and end apart: 5, of which 5 were waited for; matrix products, arithmetic and copies ran while one was open for 8% of the time, Pallas kernels for 0%

commit v1 on v0

--- a/solution.py
+++ b/solution.py
@@ -1,8 +1,11 @@
+import functools
 import math
 
 import jax
 import jax.numpy as jnp
 from jax import lax
+from jax.experimental import pallas as pl
+from jax.experimental.pallas import tpu as pltpu
 from jax.sharding import PartitionSpec as P
 
 HEADS = 40
@@ -152,6 +155,393 @@
         attended_tangent.astype(jnp.bfloat16).reshape(token_count, feature_width),
     )
 
+LINE = 4
+NEG = -1e30
+MESH = pl.DeviceIdType.MESH
+NT = (((1,), (1,)), ((), ()))
+
+
+def fused_kernel(
+    heads,
+    shares,
+    full_width,
+    raw_ref,
+    tan_ref,
+    gain_ref,
+    keys_ref,
+    vals_ref,
+    picked_ref,
+    out_ref,
+    dout_ref,
+    kv_in,
+    norm_out,
+    norm_in,
+    pick_all,
+    q_all,
+    part_out,
+    part_in,
+    stat_out,
+    stat_in,
+    own_part,
+    own_stat,
+    kv_send,
+    kv_recv,
+    norm_send,
+    norm_recv,
+    pick_send,
+    pick_recv,
+    q_send,
+    q_recv,
+    part_send,
+    part_recv,
+    stat_send,
+    stat_recv,
+):
+    me = lax.axis_index("mem")
+    share = lax.axis_index("pb")
+    pos, side = me // 2, lax.rem(me, 2)
+    rows = raw_ref.shape[0]
+    scale = 1.0 / math.sqrt(HDIM)
+
+    def mem_of(position):
+        return position * 2 + side
+
+    other_side = pos * 2 + (1 - side)
+    far = [lax.rem(pos + j, LINE) for j in range(1, LINE)]
+    shares_far = [lax.rem(share + j, shares) for j in range(1, shares)]
+
+    def cols(head):
+        return pl.ds(pl.multiple_of(head * HDIM, HDIM), HDIM)
+
+    barrier = pltpu.get_barrier_semaphore()
+    pl.semaphore_signal(
+        barrier, inc=1, device_id={"mem": other_side, "pb": share}, device_id_type=MESH
+    )
+    for place in far:
+        pl.semaphore_signal(
+            barrier, inc=1, device_id={"mem": mem_of(place), "pb": share}, device_id_type=MESH
+        )
+    for s in shares_far:
+        pl.semaphore_signal(barrier, inc=1, device_id={"mem": me, "pb": s}, device_id_type=MESH)
+    pl.semaphore_wait(barrier, 1 + len(far) + len(shares_far))
+
+    def remote(src, dst, send, recv, mem, pb):
+        return pltpu.make_async_remote_copy(
+            src_ref=src,
+            dst_ref=dst,
+            send_sem=send,
+            recv_sem=recv,
+            device_id={"mem": mem, "pb": pb},
+            device_id_type=MESH,
+        )
+
+    def kv_copy(which, head):
+        src = (keys_ref, vals_ref)[which].at[:, cols(head)]
+        return remote(
+            src,
+            kv_in.at[which, head],
+            kv_send.at[which, head],
+            kv_recv.at[which, head],
+            other_side,
+            share,
+        )
+
+    def norm_copy(slot, to):
+        return remote(
+            norm_out, norm_in.at[slot], norm_send.at[to], norm_recv.at[slot], me, to
+        )
+
+    def pick_copy(slot, to):
+        return remote(
+            picked_ref,
+            pick_all.at[slot],
+            pick_send.at[to],
+            pick_recv.at[slot],
+            mem_of(to),
+            share,
+        )
+
+    def q_copy(origin, head, way):
+        to = lax.rem(pos + (1 if way == 0 else LINE - 1), LINE)
+        return remote(
+            q_all.at[origin, head],
+            q_all.at[origin, head],
+            q_send.at[origin, way, head],
+            q_recv.at[origin, head],
+            mem_of(to),
+            share,
+        )
+
+    def part_copy(slot, to, head):
+        return remote(
+            part_out.at[to, head],
+            part_in.at[slot, head],
+            part_send.at[to, head],
+            part_recv.at[slot, head],
+            mem_of(to),
+            share,
+        )
+
+    def stat_copy(slot, to, head):
+        return remote(
+            stat_out.at[to, head],
+            stat_in.at[slot, head],
+            stat_send.at[to, head],
+            stat_recv.at[slot, head],
+            mem_of(to),
+            share,
+        )
+
+    def add_sums(head, carry):
+        square, cross = carry
+        raw = raw_ref[:, cols(head)].astype(jnp.float32)
+        tan = tan_ref[:, cols(head)].astype(jnp.float32)
+        return square + raw * raw, cross + raw * tan
+
+    blank = jnp.zeros((rows, HDIM), jnp.float32)
+    square, cross = lax.fori_loop(0, heads, add_sums, (blank, blank))
+    lane = lax.broadcasted_iota(jnp.int32, (rows, HDIM), 1)
+    sums = jnp.where(
+        lane == 0,
+        jnp.sum(square, axis=1, keepdims=True),
+        jnp.where(lane == 1, jnp.sum(cross, axis=1, keepdims=True), 0.0),
+    )
+    sums_t = sums.T[0:8, :]
+    norm_out[...] = sums_t
+    for s in shares_far:
+        norm_copy(share, s).start()
+    for place in far:
+        pick_copy(pos, place).start()
+
+    def start_kv(head, carry):
+        kv_copy(0, head).start()
+        kv_copy(1, head).start()
+        return carry
+
+    lax.fori_loop(0, heads, start_kv, 0)
+
+    for s in shares_far:
+        norm_copy(s, s).wait_recv()
+        sums_t = sums_t + norm_in[s]
+    sums = jnp.concatenate([sums_t] + [jnp.zeros_like(sums_t)] * (HDIM // 8 - 1), axis=0).T
+    inverse = lax.rsqrt(sums[:, 0:1] / full_width + EPSILON)
+    cross_mean = sums[:, 1:2] / full_width
+    slope = inverse**3 * cross_mean
+
+    def normalize(head, carry):
+        raw = raw_ref[:, cols(head)].astype(jnp.float32)
+        tan = tan_ref[:, cols(head)].astype(jnp.float32)
+        gain = gain_ref[:, cols(head)]
+        q_all[pos, head, 0:rows, :] = (raw * inverse * gain).astype(jnp.bfloat16)
+        q_all[pos, head, rows : 2 * rows, :] = (gain * (tan * inverse - raw * slope)).astype(
+            jnp.bfloat16
+        )
+
+        @pl.when(pos < LINE - 1)
+        def _():
+            q_copy(pos, head, 0).start()
+
+        @pl.when(pos > 0)
+        def _():
+            q_copy(pos, head, 1).start()
+
+        return carry
+
+    lax.fori_loop(0, heads, normalize, 0)
+
+    for place in far:
+        pick_copy(place, place).wait_recv()
+
+    def forward(head, hop):
+        @pl.when(pos >= hop)
+        def _():
+            q_copy(pos - hop, head, 0).wait_recv()
+
+            @pl.when(pos < LINE - 1)
+            def _():
+                q_copy(pos - hop, head, 0).start()
+
+        @pl.when(pos < LINE - hop)
+        def _():
+            q_copy(pos + hop, head, 1).wait_recv()
+
+            @pl.when(pos > 0)
+            def _():
+                q_copy(pos + hop, head, 1).start()
+
+    frame_row = lax.broadcasted_iota(jnp.int32, (8, rows), 0)
+
+    def compute(head):
+        kv_copy(0, head).wait_recv()
+        kv_copy(1, head).wait_recv()
+        frames = (
+            (me, keys_ref[:, cols(head)], vals_ref[:, cols(head)].T),
+            (other_side, kv_in[0, head], kv_in[1, head].T),
+        )
+        for place in far + [pos]:
+            query = q_all[place, head]
+            masks = picked_ref[...] if place is pos else pick_all[place]
+            got = []
+            for frame, keys, vals_t in frames:
+                both = lax.dot_general(keys, query, NT, preferred_element_type=jnp.float32) * scale
+                score, dscore = both[:, 0:rows], both[:, rows : 2 * rows]
+                peak = jnp.max(score, axis=0, keepdims=True)
+                weight = jnp.exp(score - peak)
+                drift = weight * dscore
+                mixed = jnp.concatenate(
+                    [weight.astype(jnp.bfloat16), drift.astype(jnp.bfloat16)], axis=1
+                )
+                part = jnp.dot(vals_t, mixed, preferred_element_type=jnp.float32)
+                mask = jnp.sum(jnp.where(frame_row == frame, masks, 0.0), axis=0, keepdims=True)
+                got.append(
+                    (
+                        mask,
+                        jnp.where(mask > 0.0, peak, NEG),
+                        jnp.sum(weight, axis=0, keepdims=True),
+                        jnp.sum(drift, axis=0, keepdims=True),
+                        part.astype(jnp.bfloat16).astype(jnp.float32),
+                    )
+                )
+            top = jnp.maximum(got[0][1], got[1][1])
+            fs = [jnp.exp(g[1] - top) * g[0] for g in got]
+            total = fs[0] * got[0][2] + fs[1] * got[1][2]
+            drift_total = fs[0] * got[0][3] + fs[1] * got[1][3]
+            merged = fs[0] * got[0][4][:, 0:rows] + fs[1] * got[1][4][:, 0:rows]
+            tangent = fs[0] * got[0][4][:, rows:] + fs[1] * got[1][4][:, rows:]
+            shift = got[0][0] * got[1][0] * drift_total / jnp.maximum(total, 0.5)
+            if place is pos:
+                shift = jnp.zeros_like(shift)
+            stats = jnp.concatenate(
+                [top, total, drift_total, shift, jnp.zeros((4, rows), jnp.float32)], axis=0
+            )
+            if place is pos:
+                own_part[head, :, 0:rows] = merged
+                own_part[head, :, rows:] = tangent
+                own_stat[head] = stats
+            else:
+                part_out[place, head, :, 0:rows] = merged.astype(jnp.bfloat16)
+                part_out[place, head, :, rows:] = (tangent - shift * merged).astype(jnp.bfloat16)
+                stat_out[place, head] = stats
+                part_copy(pos, place, head).start()
+                stat_copy(pos, place, head).start()
+
+    def merge(head):
+        parts, stats = [own_part[head]], [own_stat[head]]
+        for place in far:
+            part_copy(place, place, head).wait_recv()
+            stat_copy(place, place, head).wait_recv()
+            parts.append(part_in[place, head].astype(jnp.float32))
+            stats.append(stat_in[place, head])
+        top = functools.reduce(jnp.maximum, [s[0:1] for s in stats])
+        total = drift_total = jnp.zeros_like(top)
+        merged = tangent = jnp.zeros((HDIM, rows), jnp.float32)
+        for part, stat in zip(parts, stats):
+            factor = jnp.exp(stat[0:1] - top)
+            total += factor * stat[1:2]
+            drift_total += factor * stat[2:3]
+            merged += factor * part[:, 0:rows]
+            tangent += factor * (part[:, rows:] + stat[3:4] * part[:, 0:rows])
+        attended = merged / total
+        attended_tangent = tangent / total - drift_total / total * attended
+        out_ref[:, cols(head)] = attended.T.astype(jnp.bfloat16)
+        dout_ref[:, cols(head)] = attended_tangent.T.astype(jnp.bfloat16)
+
+    lag = 2
+
+    def step(t, carry):
+        @pl.when(t < heads)
+        def _():
+            forward(t, 1)
+
+        @pl.when((t >= 1) & (t < heads + 1))
+        def _():
+            forward(t - 1, 2)
+
+        @pl.when((t >= 2) & (t < heads + 2))
+        def _():
+            forward(t - 2, 3)
+            compute(t - 2)
+
+        @pl.when(t >= 2 + lag)
+        def _():
+            merge(t - 2 - lag)
+
+        return carry
+
+    lax.fori_loop(0, heads + 2 + lag, step, 0)
+
+    for s in shares_far:
+        norm_copy(share, s).wait_send()
+    for place in far:
+        pick_copy(pos, place).wait_send()
+
+    def drain(head, carry):
+        kv_copy(0, head).wait_send()
+        kv_copy(1, head).wait_send()
+        for place in far:
+            part_copy(pos, place, head).wait_send()
+            stat_copy(pos, place, head).wait_send()
+        for hop in range(LINE - 1):
+
+            @pl.when((pos >= hop) & (pos < LINE - 1))
+            def _():
+                q_copy(pos - hop, head, 0).wait_send()
+
+            @pl.when((pos < LINE - hop) & (pos > 0))
+            def _():
+                q_copy(pos + hop, head, 1).wait_send()
+
+        return carry
+
+    lax.fori_loop(0, heads, drain, 0)
+
+
+def dense_local(query_raw, query_tangent, norm_gain, mem_keys, mem_values, retrieved):
+    shares = lax.axis_size("pb")
+    owners = lax.axis_size("mem")
+    rows, width = query_raw.shape
+    frame = mem_keys.shape[0]
+    heads = width // HDIM
+    named = jnp.arange(owners, dtype=jnp.int32)[:, None, None] == retrieved[None]
+    picked = jnp.repeat(jnp.any(named, axis=2), QBLK, axis=1).astype(jnp.float32)
+    vmem = pl.BlockSpec(memory_space=pltpu.VMEM)
+    dma = pltpu.SemaphoreType.DMA
+    f32, bf16 = jnp.float32, jnp.bfloat16
+    return pl.pallas_call(
+        functools.partial(fused_kernel, heads, shares, width * shares),
+        out_shape=(jax.ShapeDtypeStruct((rows, width), bf16),) * 2,
+        in_specs=[vmem] * 6,
+        out_specs=(vmem, vmem),
+        scratch_shapes=[
+            pltpu.VMEM((2, heads, frame, HDIM), bf16),
+            pltpu.VMEM((8, rows), f32),
+            pltpu.VMEM((shares, 8, rows), f32),
+            pltpu.VMEM((LINE, owners, rows), f32),
+            pltpu.VMEM((LINE, heads, 2 * rows, HDIM), bf16),
+            pltpu.VMEM((LINE, heads, HDIM, 2 * rows), bf16),
+            pltpu.VMEM((LINE, heads, HDIM, 2 * rows), bf16),
+            pltpu.VMEM((LINE, heads, 8, rows), f32),
+            pltpu.VMEM((LINE, heads, 8, rows), f32),
+            pltpu.VMEM((heads, HDIM, 2 * rows), f32),
+            pltpu.VMEM((heads, 8, rows), f32),
+            dma((2, heads)),
+            dma((2, heads)),
+            dma((shares,)),
+            dma((shares,)),
+            dma((LINE,)),
+            dma((LINE,)),
+            dma((LINE, 2, heads)),
+            dma((LINE, heads)),
+            dma((LINE, heads)),
+            dma((LINE, heads)),
+            dma((LINE, heads)),
+            dma((LINE, heads)),
+        ],
+        compiler_params=pltpu.CompilerParams(
+            collective_id=0, has_side_effects=True, vmem_limit_bytes=48 * 2**20
+        ),
+    )(query_raw, query_tangent, norm_gain.reshape(1, width), mem_keys, mem_values, picked)
+
 
 def solution(mesh):
     placed = (
@@ -162,8 +552,9 @@
         P("mem", "pb"),
         P("mem", None),
     )
+    dense = mesh.shape["mem"] == 2 * LINE
     return jax.shard_map(
-        local,
+        dense_local if dense else local,
         mesh=mesh,
         in_specs=placed,
         out_specs=(P("mem", "pb"), P("mem", "pb")),

time: 411 us -> 112 us (0.27)
  waiting for transfers between devices: 156 us -> 0 us
  Pallas kernels: 0 us -> 104 us
  blocking collectives: 78.4 us -> 0 us
  matrix products: 74.6 us -> 0 us
  local copies, waits for them, and re-layouts: 64 us -> 6.88 us
  starting transfers between devices: 21 us -> 0 us
  other arithmetic: 13 us -> 0.7 us
    all_to_all x5 -> x0, waiting for transfers between devices: 156 us -> none  [the longest x1 59 us: local(): lax.all_to_all(send_tangent, 'mem', split_axis=0, concat_axis=0, tiled=True)]
    pallas_call x0 -> x1, Pallas kernels: none -> 104 us  [dense_local(): pl.pallas_call(functools.partial(fused_kernel, heads, shares, width * sha...]
    dot_general x40 -> x0, matrix products: 74.6 us -> none  [the longest x10 22.3 us: head_step(): jnp.dot(weights.astype(jnp.bfloat16), value_head, preferred_element_type=...]
    all_to_all x2 -> x0, blocking collectives: 70 us -> none  [the longest x1 60.7 us: local(): lax.all_to_all(unflatten(tangent_part, sources, slot_rows).astype(jnp.flo...]
    scatter x2 -> x0, local copies, waits for them, and re-layouts: 23.2 us -> none  [pack(): jnp.zeros((owners * capacity, QBLK, feature_width), jnp.bfloat16).at[target]]
    all_to_all x5 -> x0, starting transfers between devices: 21 us -> none  [the longest x1 5.81 us: local(): lax.all_to_all(send_query, 'mem', split_axis=0, concat_axis=0, tiled=True)]
    reshape x12 -> x1, local copies, waits for them, and re-layouts: 15.6 us -> 0.7 us  [dense_local(): norm_gain.reshape(1, width)]
    gather x5 -> x0, local copies, waits for them, and re-layouts: 12.5 us -> none  [pick_rows(): return slots[target].reshape((block_count, pick_count, QBLK) + trailing)]
  transfers between devices with their start and end apart: 5 -> 0, of which waited for: 5 -> 0; matrix products, arithmetic and copies ran while one was open for 8% -> 0% of each run, Pallas kernels for 0% -> 0%
where the time goes in v1:
time: 112 us
  Pallas kernels  104 us (93%)
  local copies, waits for them, and re-layouts  6.88 us (6%)
    pallas_call x1, Pallas kernels, dense_local(): pl.pallas_call(functools.partial(fused_kernel, heads, shares, width * sha...  104 us
    unnamed x10, local copies, waits for them, and re-layouts  6.05 us

profile of v1, /device:TPU:0, one launch (start us, length us, event | category | flops | bytes accessed | tf_op | source)
XLA Modules:
  0.0 111.8 jit_solution(14866989302438933372)
XLA Ops:
  0.6 0.7 fusion
  1.3 0.7 reshape.10.gain_ref
  2.0 0.1 copy.11
  2.2 0.0 copy-start
  2.2 1.3 %copy-done = bf16[512,1280]{1,0:T(8,128)(2,1)S(1)} copy-done((bf16[512,1280]{1,0:T(8,128)(2,1)S(1)}, bf16[512,1280]{1,0:T(8,128)(2,1)}, u32[]{:S(2)}) %copy-start) | copy-done | bytes 1310744
  3.5 0.0 copy-start.1
  3.5 1.3 %copy-done.1 = bf16[512,1280]{1,0:T(8,128)(2,1)S(1)} copy-done((bf16[512,1280]{1,0:T(8,128)(2,1)S(1)}, bf16[512,1280]{1,0:T(8,128)(2,1)}, u32[]{:S(2)}) %copy-start.1) | copy-done | bytes 1310744
  4.8 0.0 copy-start.2
  4.8 1.0 copy-done.2
  5.8 0.0 copy-start.3
  5.8 1.0 copy-done.3
  6.8 103.6 %shard_map.77 = (bf16[128,1280]{1,0:T(8,128)(2,1)S(1)}, bf16[128,1280]{1,0:T(8,128)(2,1)S(1)}) custom-call(bf16[128,1280]{1,0:T(8,128)(2,1)S(1)} %copy-done.2, bf16[128,1280]{1,0:T(8,128)(2,1)S(1)} %copy-done.3, f32[1,1280]{1,0:T(1,128)S(1)} %reshape.10.gain_ref, bf16[512,1280]{1,0:T(8,128)(2,1)S(1)} %copy-done, bf16[512,1280]{1,0:T(8,128)(2,1)S(1)} %copy-done.1, ...), custom_call_target="tpu_custom_call" | custom-call | tf_op jit(solution)/shard_map/pallas_call | solution.py:510
  110.3 0.7 copy.15
  111.1 0.7 copy.16
  (3 shorter events, 0.1 us)
Async XLA Ops:
  2.2 1.3 %copy-start = (bf16[512,1280]{1,0:T(8,128)(2,1)S(1)}, bf16[512,1280]{1,0:T(8,128)(2,1)}, u32[]{:S(2)}) copy-start(bf16[512,1280]{1,0:T(8,128)(2,1)} %keys_ref.1) | copy-start | bytes 3932164
  3.5 1.3 %copy-start.1 = (bf16[512,1280]{1,0:T(8,128)(2,1)S(1)}, bf16[512,1280]{1,0:T(8,128)(2,1)}, u32[]{:S(2)}) copy-start(bf16[512,1280]{1,0:T(8,128)(2,1)} %vals_ref.1) | copy-start | bytes 3932164
  4.8 1.0 copy-start.2
  5.8 1.0 copy-start.3

commit v2 on v1

--- a/solution.py
+++ b/solution.py
@@ -157,6 +157,8 @@
 
 LINE = 4
 NEG = -1e30
+AHEAD = 4
+LEAD = 2
 MESH = pl.DeviceIdType.MESH
 NT = (((1,), (1,)), ((), ()))
 
@@ -272,24 +274,25 @@
             share,
         )
 
-    def part_copy(slot, to, head):
-        return remote(
-            part_out.at[to, head],
-            part_in.at[slot, head],
-            part_send.at[to, head],
-            part_recv.at[slot, head],
-            mem_of(to),
-            share,
-        )
-
-    def stat_copy(slot, to, head):
-        return remote(
-            stat_out.at[to, head],
-            stat_in.at[slot, head],
-            stat_send.at[to, head],
-            stat_recv.at[slot, head],
-            mem_of(to),
-            share,
+    def part_copies(way, dest, head):
+        to = mem_of(lax.rem(pos + (1 if way == 0 else LINE - 1), LINE))
+        return (
+            remote(
+                part_out.at[dest, head],
+                part_in.at[way, dest, head],
+                part_send.at[dest, head],
+                part_recv.at[way, dest, head],
+                to,
+                share,
+            ),
+            remote(
+                stat_out.at[dest, head],
+                stat_in.at[way, dest, head],
+                stat_send.at[dest, head],
+                stat_recv.at[way, dest, head],
+                to,
+                share,
+            ),
         )
 
     def add_sums(head, carry):
@@ -313,12 +316,25 @@
     for place in far:
         pick_copy(pos, place).start()
 
-    def start_kv(head, carry):
+    def start_kv(head):
         kv_copy(0, head).start()
         kv_copy(1, head).start()
-        return carry
-
-    lax.fori_loop(0, heads, start_kv, 0)
+
+    stat_row0 = jnp.where(
+        lax.broadcasted_iota(jnp.int32, (heads, 8, rows), 1) == 0, 1.0, 0.0
+    )
+    for head in range(min(AHEAD, heads)):
+        start_kv(head)
+
+    @pl.when(pos == 0)
+    def _():
+        part_in[0, 0] = jnp.zeros_like(part_in[0, 0])
+        stat_in[0, 0] = jnp.full_like(stat_in[0, 0], NEG) * stat_row0
+
+    @pl.when(pos == LINE - 1)
+    def _():
+        part_in[1, LINE - 1] = jnp.zeros_like(part_in[1, LINE - 1])
+        stat_in[1, LINE - 1] = jnp.full_like(stat_in[1, LINE - 1], NEG) * stat_row0
 
     for s in shares_far:
         norm_copy(s, s).wait_recv()
@@ -336,7 +352,9 @@
         q_all[pos, head, rows : 2 * rows, :] = (gain * (tan * inverse - raw * slope)).astype(
             jnp.bfloat16
         )
-
+        return carry
+
+    def start_q(head):
         @pl.when(pos < LINE - 1)
         def _():
             q_copy(pos, head, 0).start()
@@ -345,9 +363,10 @@
         def _():
             q_copy(pos, head, 1).start()
 
-        return carry
-
-    lax.fori_loop(0, heads, normalize, 0)
+    for head in range(min(LEAD, heads)):
+        normalize(head, 0)
+        start_q(head)
+    lax.fori_loop(min(LEAD, heads), heads, normalize, 0)
 
     for place in far:
         pick_copy(place, place).wait_recv()
@@ -408,67 +427,112 @@
             drift_total = fs[0] * got[0][3] + fs[1] * got[1][3]
             merged = fs[0] * got[0][4][:, 0:rows] + fs[1] * got[1][4][:, 0:rows]
             tangent = fs[0] * got[0][4][:, rows:] + fs[1] * got[1][4][:, rows:]
-            shift = got[0][0] * got[1][0] * drift_total / jnp.maximum(total, 0.5)
-            if place is pos:
-                shift = jnp.zeros_like(shift)
-            stats = jnp.concatenate(
-                [top, total, drift_total, shift, jnp.zeros((4, rows), jnp.float32)], axis=0
+            own_part[place, head, :, 0:rows] = merged
+            own_part[place, head, :, rows:] = tangent
+            own_stat[place, head] = jnp.concatenate(
+                [top, total, drift_total, jnp.zeros((5, rows), jnp.float32)], axis=0
             )
-            if place is pos:
-                own_part[head, :, 0:rows] = merged
-                own_part[head, :, rows:] = tangent
-                own_stat[head] = stats
-            else:
-                part_out[place, head, :, 0:rows] = merged.astype(jnp.bfloat16)
-                part_out[place, head, :, rows:] = (tangent - shift * merged).astype(jnp.bfloat16)
-                stat_out[place, head] = stats
-                part_copy(pos, place, head).start()
-                stat_copy(pos, place, head).start()
+
+    def held(dest, head):
+        stat = own_stat[dest, head]
+        return stat[0:1], stat[1:2], stat[2:3], own_part[dest, head]
+
+    def joined(have, way, dest, head):
+        stat = stat_in[way, dest, head]
+        unit = jnp.concatenate([stat[3:4], stat[4:5]], axis=1)
+        part = part_in[way, dest, head].astype(jnp.int32).astype(jnp.float32) * unit
+        top = jnp.maximum(have[0], stat[0:1])
+        fa, fb = jnp.exp(have[0] - top), jnp.exp(stat[0:1] - top)
+        return (
+            top,
+            fa * have[1] + fb * stat[1:2],
+            fa * have[2] + fb * stat[2:3],
+            jnp.concatenate([fa, fa], axis=1) * have[3]
+            + jnp.concatenate([fb, fb], axis=1) * part,
+        )
+
+    def send_on(lag, way, dest, head):
+        have = held(dest, head)
+        if lag > 0:
+            for copy in part_copies(way, dest, head):
+                copy.wait_recv()
+            have = joined(have, way, dest, head)
+        top, total, drift_total, part = have
+        unit = jnp.maximum(jnp.max(jnp.abs(part), axis=0, keepdims=True), 1e-25) / 32767.0
+        coded = jnp.round(part * (1.0 / unit))
+        part_out[dest, head] = coded.astype(jnp.int32).astype(jnp.int16)
+        stat_out[dest, head] = jnp.concatenate(
+            [
+                top,
+                total,
+                drift_total,
+                unit[:, 0:rows],
+                unit[:, rows:],
+                jnp.zeros((3, rows), jnp.float32),
+            ],
+            axis=0,
+        )
+        for copy in part_copies(way, dest, head):
+            copy.start()
+
+    def relay(lag, head):
+        @pl.when(pos == lag)
+        def _():
+            for dest in range(LINE - 1, lag, -1):
+                send_on(lag, 0, dest, head)
+
+        @pl.when(pos == LINE - 1 - lag)
+        def _():
+            for dest in range(LINE - 1 - lag):
+                send_on(lag, 1, dest, head)
 
     def merge(head):
-        parts, stats = [own_part[head]], [own_stat[head]]
-        for place in far:
-            part_copy(place, place, head).wait_recv()
-            stat_copy(place, place, head).wait_recv()
-            parts.append(part_in[place, head].astype(jnp.float32))
-            stats.append(stat_in[place, head])
-        top = functools.reduce(jnp.maximum, [s[0:1] for s in stats])
-        total = drift_total = jnp.zeros_like(top)
-        merged = tangent = jnp.zeros((HDIM, rows), jnp.float32)
-        for part, stat in zip(parts, stats):
-            factor = jnp.exp(stat[0:1] - top)
-            total += factor * stat[1:2]
-            drift_total += factor * stat[2:3]
-            merged += factor * part[:, 0:rows]
-            tangent += factor * (part[:, rows:] + stat[3:4] * part[:, 0:rows])
-        attended = merged / total
-        attended_tangent = tangent / total - drift_total / total * attended
+        @pl.when(pos > 0)
+        def _():
+            for copy in part_copies(0, pos, head):
+                copy.wait_recv()
+
+        @pl.when(pos < LINE - 1)
+        def _():
+            for copy in part_copies(1, pos, head):
+                copy.wait_recv()
+
+        have = joined(joined(held(pos, head), 0, pos, head), 1, pos, head)
+        _top, total, drift_total, part = have
+        attended = part[:, 0:rows] / total
+        attended_tangent = part[:, rows:] / total - drift_total / total * attended
         out_ref[:, cols(head)] = attended.T.astype(jnp.bfloat16)
         dout_ref[:, cols(head)] = attended_tangent.T.astype(jnp.bfloat16)
 
-    lag = 2
-
     def step(t, carry):
-        @pl.when(t < heads)
-        def _():
-            forward(t, 1)
-
-        @pl.when((t >= 1) & (t < heads + 1))
-        def _():
-            forward(t - 1, 2)
-
-        @pl.when((t >= 2) & (t < heads + 2))
-        def _():
-            forward(t - 2, 3)
-            compute(t - 2)
-
-        @pl.when(t >= 2 + lag)
-        def _():
-            merge(t - 2 - lag)
-
+        @pl.when(t + AHEAD < heads)
+        def _():
+            start_kv(t + AHEAD)
+
+        @pl.when(t + LEAD < heads)
+        def _():
+            start_q(t + LEAD)
+
+        def staged(behind, run):
+            @pl.when((t >= behind) & (t < heads + behind))
+            def _():
+                run(t - behind)
+
+        staged(0, lambda head: forward(head, 1))
+        staged(1, lambda head: forward(head, 2))
+        staged(3, lambda head: relay(1, head))
+        staged(4, lambda head: relay(2, head))
+
+        def main(head):
+            forward(head, 3)
+            compute(head)
+            relay(0, head)
+
+        staged(2, main)
+        staged(5, merge)
         return carry
 
-    lax.fori_loop(0, heads + 2 + lag, step, 0)
+    lax.fori_loop(0, heads + 5, step, 0)
 
     for s in shares_far:
         norm_copy(share, s).wait_send()
@@ -479,8 +543,8 @@
         kv_copy(0, head).wait_send()
         kv_copy(1, head).wait_send()
         for place in far:
-            part_copy(pos, place, head).wait_send()
-            stat_copy(pos, place, head).wait_send()
+            for copy in part_copies(0, place, head):
+                copy.wait_send()
         for hop in range(LINE - 1):
 
             @pl.when((pos >= hop) & (pos < LINE - 1))
@@ -518,12 +582,12 @@
             pltpu.VMEM((shares, 8, rows), f32),
             pltpu.VMEM((LINE, owners, rows), f32),
             pltpu.VMEM((LINE, heads, 2 * rows, HDIM), bf16),
-            pltpu.VMEM((LINE, heads, HDIM, 2 * rows), bf16),
-            pltpu.VMEM((LINE, heads, HDIM, 2 * rows), bf16),
+            pltpu.VMEM((LINE, heads, HDIM, 2 * rows), jnp.int16),
+            pltpu.VMEM((2, LINE, heads, HDIM, 2 * rows), jnp.int16),
             pltpu.VMEM((LINE, heads, 8, rows), f32),
+            pltpu.VMEM((2, LINE, heads, 8, rows), f32),
+            pltpu.VMEM((LINE, heads, HDIM, 2 * rows), f32),
             pltpu.VMEM((LINE, heads, 8, rows), f32),
-            pltpu.VMEM((heads, HDIM, 2 * rows), f32),
-            pltpu.VMEM((heads, 8, rows), f32),
             dma((2, heads)),
             dma((2, heads)),
             dma((shares,)),
@@ -533,9 +597,9 @@
             dma((LINE, 2, heads)),
             dma((LINE, heads)),
             dma((LINE, heads)),
+            dma((2, LINE, heads)),
             dma((LINE, heads)),
-            dma((LINE, heads)),
-            dma((LINE, heads)),
+            dma((2, LINE, heads)),
         ],
         compiler_params=pltpu.CompilerParams(
             collective_id=0, has_side_effects=True, vmem_limit_bytes=48 * 2**20

time: 112 us -> 97.2 us (0.87)
  Pallas kernels: 104 us -> 88.7 us
    pallas_call x1, Pallas kernels: 104 us -> 88.7 us  [dense_local(): pl.pallas_call(functools.partial(fused_kernel, heads, shares, width * sha...]
where the time goes in v2:
time: 97.2 us; the launch traced here: 96.9 us
  Pallas kernels  88.7 us (91%)
  local copies, waits for them, and re-layouts  6.88 us (7%)
    pallas_call x1, Pallas kernels, dense_local(): pl.pallas_call(functools.partial(fused_kernel, heads, shares, width * sha...  88.7 us
    unnamed x10, local copies, waits for them, and re-layouts  6.05 us

profile of v2, /device:TPU:0, one launch (start us, length us, event | category | flops | bytes accessed | tf_op | source)
XLA Modules:
  0.0 96.9 jit_solution(12059070074773871382)
XLA Ops:
  0.6 0.7 fusion
  1.3 0.7 reshape.10.gain_ref
  2.0 0.1 copy.11
  2.2 0.0 copy-start
  2.2 1.3 %copy-done = bf16[512,1280]{1,0:T(8,128)(2,1)S(1)} copy-done((bf16[512,1280]{1,0:T(8,128)(2,1)S(1)}, bf16[512,1280]{1,0:T(8,128)(2,1)}, u32[]{:S(2)}) %copy-start) | copy-done | bytes 1310744
  3.5 0.0 copy-start.1
  3.5 1.3 %copy-done.1 = bf16[512,1280]{1,0:T(8,128)(2,1)S(1)} copy-done((bf16[512,1280]{1,0:T(8,128)(2,1)S(1)}, bf16[512,1280]{1,0:T(8,128)(2,1)}, u32[]{:S(2)}) %copy-start.1) | copy-done | bytes 1310744
  4.8 0.0 copy-start.2
  4.8 1.0 %copy-done.2 = bf16[128,1280]{1,0:T(8,128)(2,1)S(1)} copy-done((bf16[128,1280]{1,0:T(8,128)(2,1)S(1)}, bf16[128,1280]{1,0:T(8,128)(2,1)}, u32[]{:S(2)}) %copy-start.2) | copy-done | bytes 327704
  5.8 0.0 copy-start.3
  5.8 1.0 %copy-done.3 = bf16[128,1280]{1,0:T(8,128)(2,1)S(1)} copy-done((bf16[128,1280]{1,0:T(8,128)(2,1)S(1)}, bf16[128,1280]{1,0:T(8,128)(2,1)}, u32[]{:S(2)}) %copy-start.3) | copy-done | bytes 327704
  6.8 88.7 %shard_map.77 = (bf16[128,1280]{1,0:T(8,128)(2,1)S(1)}, bf16[128,1280]{1,0:T(8,128)(2,1)S(1)}) custom-call(bf16[128,1280]{1,0:T(8,128)(2,1)S(1)} %copy-done.2, bf16[128,1280]{1,0:T(8,128)(2,1)S(1)} %copy-done.3, f32[1,1280]{1,0:T(1,128)S(1)} %reshape.10.gain_ref, bf16[512,1280]{1,0:T(8,128)(2,1)S(1)} %copy-done, bf16[512,1280]{1,0:T(8,128)(2,1)S(1)} %copy-done.1, ...), custom_call_target="tpu_custom_call" | custom-call | tf_op jit(solution)/shard_map/pallas_call | solution.py:574
  95.5 0.7 copy.15
  96.2 0.7 copy.16
  (3 shorter events, 0.1 us)
Async XLA Ops:
  2.2 1.3 %copy-start = (bf16[512,1280]{1,0:T(8,128)(2,1)S(1)}, bf16[512,1280]{1,0:T(8,128)(2,1)}, u32[]{:S(2)}) copy-start(bf16[512,1280]{1,0:T(8,128)(2,1)} %keys_ref.1) | copy-start | bytes 3932164
  3.5 1.3 %copy-start.1 = (bf16[512,1280]{1,0:T(8,128)(2,1)S(1)}, bf16[512,1280]{1,0:T(8,128)(2,1)}, u32[]{:S(2)}) copy-start(bf16[512,1280]{1,0:T(8,128)(2,1)} %vals_ref.1) | copy-start | bytes 3932164
  4.8 1.0 %copy-start.2 = (bf16[128,1280]{1,0:T(8,128)(2,1)S(1)}, bf16[128,1280]{1,0:T(8,128)(2,1)}, u32[]{:S(2)}) copy-start(bf16[128,1280]{1,0:T(8,128)(2,1)} %raw_ref.1) | copy-start | bytes 983044
  5.8 1.0 %copy-start.3 = (bf16[128,1280]{1,0:T(8,128)(2,1)S(1)}, bf16[128,1280]{1,0:T(8,128)(2,1)}, u32[]{:S(2)}) copy-start(bf16[128,1280]{1,0:T(8,128)(2,1)} %tan_ref.1) | copy-start | bytes 983044

commit v3 on v2

--- a/solution.py
+++ b/solution.py
@@ -158,6 +158,7 @@
 LINE = 4
 NEG = -1e30
 AHEAD = 4
+LAGS = (0, 1, 2, 4, 6, 8)
 LEAD = 2
 MESH = pl.DeviceIdType.MESH
 NT = (((1,), (1,)), ((), ()))
@@ -518,21 +519,21 @@
             def _():
                 run(t - behind)
 
-        staged(0, lambda head: forward(head, 1))
-        staged(1, lambda head: forward(head, 2))
-        staged(3, lambda head: relay(1, head))
-        staged(4, lambda head: relay(2, head))
+        staged(LAGS[0], lambda head: forward(head, 1))
+        staged(LAGS[1], lambda head: forward(head, 2))
+        staged(LAGS[3], lambda head: relay(1, head))
+        staged(LAGS[4], lambda head: relay(2, head))
 
         def main(head):
             forward(head, 3)
             compute(head)
             relay(0, head)
 
-        staged(2, main)
-        staged(5, merge)
+        staged(LAGS[2], main)
+        staged(LAGS[5], merge)
         return carry
 
-    lax.fori_loop(0, heads + 5, step, 0)
+    lax.fori_loop(0, heads + LAGS[5], step, 0)
 
     for s in shares_far:
         norm_copy(share, s).wait_send()

time: 97.2 us -> 94.3 us (0.970)
  Pallas kernels: 88.7 us -> 85.8 us
    pallas_call x1, Pallas kernels: 88.7 us -> 85.8 us  [dense_local(): pl.pallas_call(functools.partial(fused_kernel, heads, shares, width * sha...]
where the time goes in v3:
time: 94.3 us; the launch traced here: 94 us
  Pallas kernels  85.8 us (91%)
  local copies, waits for them, and re-layouts  6.88 us (7%)
    pallas_call x1, Pallas kernels, dense_local(): pl.pallas_call(functools.partial(fused_kernel, heads, shares, width * sha...  85.8 us
    unnamed x10, local copies, waits for them, and re-layouts  6.05 us

profile of v3, /device:TPU:0, one launch (start us, length us, event | category | flops | bytes accessed | tf_op | source)
XLA Modules:
  0.0 94.0 jit_solution(17274318386622688950)
XLA Ops:
  0.6 0.7 fusion
  1.3 0.7 reshape.10.gain_ref
  2.0 0.1 copy.11
  2.2 0.0 copy-start
  2.2 1.3 %copy-done = bf16[512,1280]{1,0:T(8,128)(2,1)S(1)} copy-done((bf16[512,1280]{1,0:T(8,128)(2,1)S(1)}, bf16[512,1280]{1,0:T(8,128)(2,1)}, u32[]{:S(2)}) %copy-start) | copy-done | bytes 1310744
  3.5 0.0 copy-start.1
  3.5 1.3 %copy-done.1 = bf16[512,1280]{1,0:T(8,128)(2,1)S(1)} copy-done((bf16[512,1280]{1,0:T(8,128)(2,1)S(1)}, bf16[512,1280]{1,0:T(8,128)(2,1)}, u32[]{:S(2)}) %copy-start.1) | copy-done | bytes 1310744
  4.8 0.0 copy-start.2
  4.8 1.0 %copy-done.2 = bf16[128,1280]{1,0:T(8,128)(2,1)S(1)} copy-done((bf16[128,1280]{1,0:T(8,128)(2,1)S(1)}, bf16[128,1280]{1,0:T(8,128)(2,1)}, u32[]{:S(2)}) %copy-start.2) | copy-done | bytes 327704
  5.8 0.0 copy-start.3
  5.8 1.0 %copy-done.3 = bf16[128,1280]{1,0:T(8,128)(2,1)S(1)} copy-done((bf16[128,1280]{1,0:T(8,128)(2,1)S(1)}, bf16[128,1280]{1,0:T(8,128)(2,1)}, u32[]{:S(2)}) %copy-start.3) | copy-done | bytes 327704
  6.8 85.8 %shard_map.77 = (bf16[128,1280]{1,0:T(8,128)(2,1)S(1)}, bf16[128,1280]{1,0:T(8,128)(2,1)S(1)}) custom-call(bf16[128,1280]{1,0:T(8,128)(2,1)S(1)} %copy-done.2, bf16[128,1280]{1,0:T(8,128)(2,1)S(1)} %copy-done.3, f32[1,1280]{1,0:T(1,128)S(1)} %reshape.10.gain_ref, bf16[512,1280]{1,0:T(8,128)(2,1)S(1)} %copy-done, bf16[512,1280]{1,0:T(8,128)(2,1)S(1)} %copy-done.1, ...), custom_call_target="tpu_custom_call" | custom-call | tf_op jit(solution)/shard_map/pallas_call | solution.py:575
  92.6 0.7 copy.15
  93.3 0.7 copy.16
  (3 shorter events, 0.1 us)
Async XLA Ops:
  2.2 1.3 %copy-start = (bf16[512,1280]{1,0:T(8,128)(2,1)S(1)}, bf16[512,1280]{1,0:T(8,128)(2,1)}, u32[]{:S(2)}) copy-start(bf16[512,1280]{1,0:T(8,128)(2,1)} %keys_ref.1) | copy-start | bytes 3932164
  3.5 1.3 %copy-start.1 = (bf16[512,1280]{1,0:T(8,128)(2,1)S(1)}, bf16[512,1280]{1,0:T(8,128)(2,1)}, u32[]{:S(2)}) copy-start(bf16[512,1280]{1,0:T(8,128)(2,1)} %vals_ref.1) | copy-start | bytes 3932164
  4.8 1.0 %copy-start.2 = (bf16[128,1280]{1,0:T(8,128)(2,1)S(1)}, bf16[128,1280]{1,0:T(8,128)(2,1)}, u32[]{:S(2)}) copy-start(bf16[128,1280]{1,0:T(8,128)(2,1)} %raw_ref.1) | copy-start | bytes 983044
  5.8 1.0 %copy-start.3 = (bf16[128,1280]{1,0:T(8,128)(2,1)S(1)}, bf16[128,1280]{1,0:T(8,128)(2,1)}, u32[]{:S(2)}) copy-start(bf16[128,1280]{1,0:T(8,128)(2,1)} %tan_ref.1) | copy-start | bytes 983044
